TPU v7x, 128 devices: a whole 4x4x4 slice. The times are simulated.
128 devices in a mesh: seq: 32 (over z, x, core), batch: 4 (over y).
Axes of the slice: x: 4, y: 4, z: 4, core: 2. Of those that a mesh axis runs over, the one named last changes fastest.
Arguments:
- queries: bfloat16 [512, 4096], P(('batch', 'seq')), parts along dimension 0, may hold values from -720 to 720
- prompt_keys: bfloat16 [131072, 512], P(('batch', 'seq')), parts along dimension 0, may hold values from -6 to 6
- prompt_values: bfloat16 [131072, 512], P(('batch', 'seq')), parts along dimension 0, may hold values from -12 to 12
- response_keys: bfloat16 [512, 512], P(('batch', 'seq')), parts along dimension 0, may hold values from -6 to 6
- response_values: bfloat16 [512, 512], P(('batch', 'seq')), parts along dimension 0, may hold values from -12 to 12
- resp_len: int32 [4], P('batch'), parts along dimension 0, may hold values from 32 to 128
- residual: bfloat16 [512, 4096], P('batch', 'seq'), parts along dimension 0, may hold values from -6 to 6
- out_weight: bfloat16 [4096, 4096], P(None, 'seq'), may hold values from -0.09375 to 0.09375
- norm_gain: float32 [4096], P('seq'), may hold values from 0.5 to 40
- vocab_weight: bfloat16 [4096, 77824], P(None, 'seq'), may hold values from -0.25 to 0.25
- targets: int32 [512], P('batch'), parts along dimension 0, may hold values from 0 to 77823
Outputs:
- layer_out: bfloat16 [512, 4096], P('batch', 'seq'), parts along dimension 0
- row_loss: float32 [512], P('batch'), parts along dimension 0
There are 4 independent parts, one for each index of `batch`. A program takes and returns all parts, laid end to end along the dimension named above; an argument that names none is the same for every part. Nothing has to cross between parts.
All inputs are finite; a program needn't handle non-finite values.
Results may differ from a plain program's by a relative error of at most 0.01525.
Values may be sent and summed in bfloat16 or wider, within the bound.
A program may use at most 192 MiB of HBM per device.

v0:
```python
import jax
import jax.numpy as jnp
from jax import lax
from jax.sharding import PartitionSpec as P

D = 4096
QUERY_HEADS = 32
KEY_VALUE_HEADS = 4
HEAD_SIZE = 128


def merged(part, axis, combine):
    gathered = jax.tree.map(lambda a: lax.all_gather(a, axis), part)

    def take(source):
        return jax.tree.map(lambda a: lax.dynamic_index_in_dim(a, source, 0, False), gathered)

    return lax.fori_loop(
        1, lax.axis_size(axis), lambda source, state: combine(state, take(source)), take(0)
    )


def local_partials(query_stack, joined_keys, joined_values, allowed):
    row_total_count = query_stack.shape[0]
    group_count = QUERY_HEADS // KEY_VALUE_HEADS
    grouped_queries = query_stack.reshape(
        row_total_count, KEY_VALUE_HEADS, group_count, HEAD_SIZE
    ).transpose(1, 0, 2, 3)
    heads_of_keys = joined_keys.transpose(1, 0, 2)
    heads_of_values = joined_values.transpose(1, 0, 2)

    def one_group(operands):
        query_block, key_block, value_block = operands
        scores = jnp.einsum(
            "rgd,kd->rgk", query_block, key_block, preferred_element_type=jnp.float32
        ) * HEAD_SIZE ** (-0.5)
        scores = jnp.where(allowed[:, None, :], scores, -jnp.inf)
        peak = jnp.max(scores, -1)
        weights = jnp.exp(scores - peak[..., None])
        total = jnp.sum(weights, -1)
        output = jnp.einsum(
            "rgk,kd->rgd",
            weights.astype(jnp.bfloat16),
            value_block,
            preferred_element_type=jnp.float32,
        )
        return (peak, total, output)

    peak, total, output = lax.map(one_group, (grouped_queries, heads_of_keys, heads_of_values))
    peak = peak.transpose(1, 0, 2).reshape(row_total_count, QUERY_HEADS)
    total = total.transpose(1, 0, 2).reshape(row_total_count, QUERY_HEADS)
    output = output.transpose(1, 0, 2, 3).reshape(row_total_count, QUERY_HEADS, HEAD_SIZE)
    return (peak, total, output)


def join_partials(first, second):
    peak_a, total_a, output_a = first
    peak_b, total_b, output_b = second
    peak = jnp.maximum(peak_a, peak_b)
    scale_a = jnp.exp(peak_a - peak)
    scale_b = jnp.exp(peak_b - peak)
    total = total_a * scale_a + total_b * scale_b
    output = output_a * scale_a[..., None] + output_b * scale_b[..., None]
    return (peak, total, output)


def local(
    queries,
    prompt_keys,
    prompt_values,
    response_keys,
    response_values,
    resp_len,
    residual,
    out_weight,
    norm_gain,
    vocab_weight,
    targets,
):
    shards = lax.axis_size("seq")
    position = lax.axis_index("seq")
    rows_per_shard = queries.shape[0]
    row_total_count = rows_per_shard * shards
    prompt_rows = prompt_keys.shape[0]
    length = resp_len[0]
    query_stack = lax.all_gather(queries, "seq", axis=0, tiled=True)
    joined_keys = jnp.concatenate([prompt_keys, response_keys], 0).reshape(
        prompt_rows + rows_per_shard, KEY_VALUE_HEADS, HEAD_SIZE
    )
    joined_values = jnp.concatenate([prompt_values, response_values], 0).reshape(
        prompt_rows + rows_per_shard, KEY_VALUE_HEADS, HEAD_SIZE
    )
    row_ids = jnp.arange(row_total_count, dtype=jnp.int32)
    key_ids = position * rows_per_shard + jnp.arange(rows_per_shard, dtype=jnp.int32)
    resp_ok = (key_ids[None, :] <= row_ids[:, None]) & (key_ids[None, :] < length)
    allowed = jnp.concatenate([jnp.ones((row_total_count, prompt_rows), dtype=bool), resp_ok], 1)
    peak, total, output = local_partials(query_stack, joined_keys, joined_values, allowed)
    peak_all, total_all, output_all = merged((peak, total, output), "seq", join_partials)
    attn = (
        (output_all / total_all[..., None])
        .reshape(row_total_count, QUERY_HEADS * HEAD_SIZE)
        .astype(jnp.bfloat16)
    )
    projected = jnp.dot(attn, out_weight, preferred_element_type=jnp.float32)
    layer_out = (residual.astype(jnp.float32) + projected).astype(jnp.bfloat16)
    layer_float = layer_out.astype(jnp.float32)
    square_total = lax.psum(jnp.sum(layer_float * layer_float, -1), "seq")
    inverse = lax.rsqrt(square_total / D + 1e-06)
    normed = (layer_float * inverse[:, None] * norm_gain).astype(jnp.bfloat16)
    vocab_dev = vocab_weight.shape[1]
    logits = jnp.dot(
        lax.all_gather(normed, "seq", axis=1, tiled=True),
        vocab_weight,
        preferred_element_type=jnp.float32,
    )
    vocab_ids = position * vocab_dev + jnp.arange(vocab_dev, dtype=jnp.int32)
    hits = targets[:, None] == vocab_ids[None, :]
    target_part = jnp.sum(jnp.where(hits, logits, 0.0), -1)
    local_peak = jnp.max(logits, -1)
    top_logit = lax.pmax(local_peak, "seq")
    exp_total = jnp.sum(jnp.exp(logits - top_logit[:, None]), -1)
    whole_total, target_logit = lax.psum((exp_total, target_part), "seq")
    log_total = top_logit + jnp.log(whole_total)
    row_loss = jnp.where(row_ids < length, log_total - target_logit, jnp.float32(0.0))
    return (layer_out, row_loss)


def solution(mesh):
    placed = (
        P(("batch", "seq"), None),
        P(("batch", "seq"), None),
        P(("batch", "seq"), None),
        P(("batch", "seq"), None),
        P(("batch", "seq"), None),
        P("batch"),
        P("batch", "seq"),
        P(None, "seq"),
        P("seq"),
        P(None, "seq"),
        P("batch"),
    )
    return jax.shard_map(
        local,
        mesh=mesh,
        in_specs=placed,
        out_specs=(P("batch", "seq"), P("batch")),
        check_vma=False,
    )
```

profile of v0, /device:TPU:1, one launch (start us, length us, event | category | flops | bytes accessed | tf_op | source)
XLA Modules:
  0.0 685.6 jit_solution(3724428766416524031)
XLA Ops:
  14.5 42.3 %all-gather.9.cloned.1.call-done = bf16[32,4,4096]{2,1,0:T(4,128)(2,1)} async-done(((bf16[1,4,4096]{2,1,0:T(4,128)(2,1)}), bf16[32,4,4096]{2,1,0:T(4,128)(2,1)}) %all-gather.9.cloned.1.call-update) | async-done | bytes 1048592 | tf_op jit(solution)/shard_map/all_gather | solution.py:86
  59.8 16.5 %while.33 = (s32[]{:T(128)}, f32[4,128,8]{1,2,0:T(8,128)S(1)}, f32[4,128,8]{1,2,0:T(8,128)S(1)}, f32[4,128,8,128]{3,1,2,0:T(8,128)}, pred[128,1028]{0,1:T(8,128)...) while((s32[]{:T(128)}, f32[4,128,8]{1,2,0:T(8,128)S(1)}, ...), condition=%wide.region_3.4_spmd, body=%wide.region_0.3_spmd.sunk | while | flops 546334720 | bytes 14653545 | solution.py:49
  76.3 4.1 copy.53
  81.3 24.5 %all_gather.16 = f32[32,128,32]{1,2,0:T(8,128)S(1)} all-gather(f32[1,128,32]{1,2,0:T(8,128)S(1)} %bitcast.90), channel_id=1, replica_groups=mesh['seq'=32,'batch'=4] {'seq'}, dimensions={0}, use_global_device_ids=true | all-gather | bytes 540672 | tf_op jit(solution)/shard_map/all_gather | solution.py:13
  106.7 22.9 %all_gather.17 = f32[32,128,32]{1,2,0:T(8,128)S(1)} all-gather(f32[1,128,32]{1,2,0:T(8,128)S(1)} %bitcast.91), channel_id=1, replica_groups=mesh['seq'=32,'batch'=4] {'seq'}, dimensions={0}, use_global_device_ids=true | all-gather | bytes 540672 | tf_op jit(solution)/shard_map/all_gather | solution.py:13
  130.5 152.5 %all-gather.5.cloned.1.call-done = f32[32,128,32,128]{3,2,1,0:T(8,128)} async-done(((f32[1,128,32,128]{3,2,1,0:T(8,128)}), f32[32,128,32,128]{3,2,1,0:T(8,128)}) %all-gather.5.cloned.1.call-update) | async-done | bytes 67108880 | tf_op jit(solution)/shard_map/all_gather | solution.py:13
  284.8 148.7 %while.34 = (s32[]{:T(128)}, f32[128,32]{1,0:T(8,128)S(1)}, f32[128,32]{1,0:T(8,128)S(1)}, f32[128,32,128]{2,1,0:T(8,128)S(1)}, f32[32,128,32]{1,2,0:T(8,128)}, ...) while((s32[]{:T(128)}, f32[128,32]{1,0:T(8,128)S(1)}, ...), condition=%wide.region_5.6_spmd, body=%wide.region_4.5_spmd.sunk | while | flops 1597445 | bytes 6586519 | solution.py:18
  285.9 3.8 fusion.47
  290.7 3.8 fusion.47
  295.5 3.8 fusion.47
  300.3 3.8 fusion.47
  305.1 3.8 fusion.47
  309.9 3.8 fusion.47
  314.7 3.8 fusion.47
  319.4 3.8 fusion.47
  324.2 3.8 fusion.47
  329.0 3.8 fusion.47
  333.8 3.8 fusion.47
  338.6 3.8 fusion.47
  343.4 3.8 fusion.47
  348.2 3.8 fusion.47
  353.0 3.8 fusion.47
  357.8 3.8 fusion.47
  362.6 3.8 fusion.47
  367.4 3.8 fusion.47
  372.2 3.8 fusion.47
  410.6 3.8 fusion.47
  435.0 62.5 %psum.21 = f32[128]{0:T(128)S(1)} all-reduce(f32[128]{0:T(128)S(1)} %get-tuple-element.308), channel_id=1, replica_groups=mesh['seq'=32,'batch'=4] {'seq'}, use_global_device_ids=true, to_apply=%region_7.8 | all-reduce | flops 128 | bytes 1024 | tf_op jit(solution)/shard_map/psum | solution.py:107
  498.9 41.7 %all-gather.7.cloned.1.call-done = bf16[128,4096]{0,1:T(8,128)(2,1)} async-done(((bf16[128,128]{0,1:T(8,128)(2,1)}), bf16[128,4096]{0,1:T(8,128)(2,1)}) %all-gather.7.cloned.1.call-update) | async-done | bytes 1048592 | tf_op jit(solution)/shard_map/all_gather | solution.py:112
  540.7 10.0 %fusion.30 = (f32[128]{0:T(128)S(1)}, f32[128,2432]{1,0:T(8,128)S(1)}) fusion(bf16[128,4096]{0,1:T(8,128)(2,1)} %all-gather.7.cloned.1.call-done, bf16[4096,2432]{1,0:T(8,128)(2,1)} %param.24), kind=kOutput, calls=%fused_computation.55 | convolution fusion | flops 2550448128 | bytes 22217216 | tf_op jit(solution)/shard_map/dot_general | solution.py:111
  550.6 62.3 %pmax.7 = f32[128]{0:T(128)S(1)} all-reduce(f32[128]{0:T(128)S(1)} %get-tuple-element.310), channel_id=1, replica_groups=mesh['seq'=32,'batch'=4] {'seq'}, use_global_device_ids=true, to_apply=%region_9.10 | all-reduce | flops 128 | bytes 1024 | tf_op jit(solution)/shard_map/pmax | solution.py:120
  613.4 65.2 %all-reduce.1 = (f32[128]{0:T(128)S(1)}, f32[128]{0:T(128)S(1)}) all-reduce(f32[128]{0:T(128)S(1)} %get-tuple-element.265, f32[128]{0:T(128)S(1)} %get-tuple-element.264), channel_id=1, replica_groups=mesh['seq'=32,'batch'=4] {'seq'}, use_global_device_ids=true, to_apply=%region_13.14 | all-reduce | flops 256 | bytes 2048 | tf_op jit(solution)/shard_map/psum | solution.py:122
  (205 shorter events, 106.6 us)
Async XLA Ops:
  7.2 427.2 %copy-start = (bf16[4096,128]{1,0:T(8,128)(2,1)S(1)}, bf16[4096,128]{1,0:T(8,128)(2,1)}, u32[]{:S(2)}) copy-start(bf16[4096,128]{1,0:T(8,128)(2,1)} %param.22) | copy-start | bytes 3145732
  7.2 49.6 %all-gather.9.cloned.1.call-start = ((), (), s32[]{:S(2)}) async-start(), calls=%async_computation.2 | async-start | bytes 1081344 | tf_op jit(solution)/shard_map/all_gather | solution.py:86
  7.9 275.2 %all-gather.5.cloned.1.call-start = ((), (), s32[]{:S(2)}) async-start(), calls=%async_computation | async-start | bytes 69206016 | tf_op jit(solution)/shard_map/all_gather | solution.py:13
  10.0 0.7 copy-start.5
  10.3 1.2 copy-start.1
  80.5 0.8 copy-start.4
  80.5 460.2 %all-gather.7.cloned.1.call-start = ((), (), s32[]{:S(2)}) async-start(), calls=%async_computation.1 | async-start | bytes 1081344 | tf_op jit(solution)/shard_map/all_gather | solution.py:112
  105.8 0.8 copy-start.2
  129.6 0.8 copy-start.3
  433.6 63.9 %copy-start.7 = (f32[128]{0:T(128)S(1)}, f32[128]{0:T(128)}, u32[]{:S(2)}) copy-start(f32[128]{0:T(128)} %param.23) | copy-start | bytes 1540
  498.9 114.0 %copy-start.6 = (s32[128]{0:T(128)S(1)}, s32[128]{0:T(128)}, u32[]{:S(2)}) copy-start(s32[128]{0:T(128)} %param.25) | copy-start | bytes 1540
Sparse Core Ops, SparseCore 0:
  10.3 46.5 all-gather.8
  80.6 202.4 all-gather.4
  498.3 42.2 all-gather.6
where the time goes:
time: 692 us; the launch traced here: 686 us
  waiting for transfers between devices  237 us (34%)
  blocking collectives  237 us (34%)
  other arithmetic  125 us (18%)
  local copies, waits for them, and re-layouts  49.5 us (7%)
  matrix products  20.9 us (3%)
  between operations  14.6 us (2%)
    all_gather x1, waiting for transfers between devices, merged(): gathered = jax.tree.map(lambda a: lax.all_gather(a, axis), part)  153 us
    add x31, other arithmetic, join_partials(): output = output_a * scale_a[..., None] + output_b * scale_b[..., None]  117 us
    psum x1, blocking collectives, local(): whole_total, target_logit = lax.psum((exp_total, target_part), 'seq')  65.2 us
    psum x1, blocking collectives, local(): square_total = lax.psum(jnp.sum(layer_float * layer_float, -1), 'seq')  62.5 us
    pmax x1, blocking collectives, local(): top_logit = lax.pmax(local_peak, 'seq')  62.3 us
    all_gather x2, blocking collectives, merged(): gathered = jax.tree.map(lambda a: lax.all_gather(a, axis), part)  47.4 us
    all_gather x1, waiting for transfers between devices, local(): query_stack = lax.all_gather(queries, 'seq', axis=0, tiled=True)  42.3 us
    all_gather x1, waiting for transfers between devices, local(): lax.all_gather(normed, 'seq', axis=1, tiled=True)  41.7 us
  transfers between devices with their start and end apart: 3, of which 3 were waited for; matrix products, arithmetic and copies ran while one was open for 1% of the time, Pallas kernels for 0%

commit v1 on v0

v1 whole, which is shorter than its diff:
```python
import functools

import jax
import jax.numpy as jnp
from jax import lax
from jax.experimental import pallas as pl
from jax.experimental.pallas import tpu as pltpu
from jax.sharding import PartitionSpec as P

D = 4096
KEY_VALUE_HEADS = 4
HEAD_SIZE = 128
ROWS = 128
VOCAB_DEV = 2432
KEYS_DEV = 1024
LOG2E = 1.4426950408889634
SCORE_SCALE = LOG2E * HEAD_SIZE ** (-0.5)
MESH = pl.DeviceIdType.MESH
PLANE_ORDER = (0, 1, 3, 2)
PLANE_BACK = (0, 2, 1, 3)
F32 = jnp.float32
BF16 = jnp.bfloat16


def dot_nt(a, b):
    return lax.dot_general(a, b, (((1,), (1,)), ((), ())), preferred_element_type=F32)


def dot_nn(a, b):
    return jnp.dot(a, b, preferred_element_type=F32)


def eye_mask():
    return lax.broadcasted_iota(jnp.int32, (128, 128), 0) == lax.broadcasted_iota(
        jnp.int32, (128, 128), 1
    )


def to_row(column):
    return jnp.sum(jnp.where(eye_mask(), column, 0.0), axis=0, keepdims=True)


def to_column(row):
    return jnp.sum(jnp.where(eye_mask(), row, 0.0), axis=1, keepdims=True)


def drain(ref, sem):
    pltpu.make_async_copy(ref, ref, sem).wait()


def kernel(
    small, prompt_keys, prompt_values, length, residual, out_weight, gain, vocab_weight, targets,
    layer_out, row_loss,
    kbuf, vbuf, krb, vrb, qbuf, ostage, sstage, rbuf, rstat, mrg, abuf, wbuf, pown, ppart,
    gbuf, ssbuf, wv, acc, fbuf,
    local_sem, vocab_sem, kv_recv, w_recv, small_recv, q_recv, r_recv, own_sem, a_recv, p_recv,
    g_recv, h_recv, s_recv, f_recv, send_sem,
):
    me = lax.axis_index("seq")
    z, x, c = me // 8, (me // 2) % 4, me % 2
    chip = me // 2
    other = 1 - c
    sibling = chip * 2 + other

    def rel_chip(dz, dx):
        return lax.rem(z + dz, 4) * 4 + lax.rem(x + dx, 4)

    def send(src, dst, sem, target, kind):
        pltpu.make_async_remote_copy(
            src_ref=src, dst_ref=dst, send_sem=send_sem.at[kind], recv_sem=sem,
            device_id={"seq": target}, device_id_type=MESH,
        ).start()

    my_cols = pl.ds(pl.multiple_of(c * 256, 256), 256)
    other_cols = pl.ds(pl.multiple_of(other * 256, 256), 256)
    my_half = pl.ds(pl.multiple_of(c * 2048, 2048), 2048)
    other_half = pl.ds(pl.multiple_of(other * 2048, 2048), 2048)
    w_lane = pl.ds(pl.multiple_of(c * 128, 128), 128)

    barrier = pltpu.get_barrier_semaphore()

    def greet(i, carry):
        pl.semaphore_signal(
            barrier, inc=1, device_id={"seq": lax.rem(me + i, 32)}, device_id_type=MESH
        )
        return carry

    lax.fori_loop(1, 32, greet, 0)

    own_copies = [
        pltpu.make_async_copy(prompt_keys.at[:, my_cols], kbuf.at[c], local_sem.at[0]),
        pltpu.make_async_copy(prompt_values.at[:, my_cols], vbuf.at[c], local_sem.at[1]),
        pltpu.make_async_copy(out_weight.at[my_half, :], wbuf.at[:, w_lane], local_sem.at[2]),
    ]
    for copy in own_copies:
        copy.start()
    vocab_copies = [
        pltpu.make_async_copy(
            vocab_weight.at[pl.ds(i * 1024, 1024), :], wv.at[pl.ds(i * 1024, 1024), :],
            vocab_sem.at[i],
        )
        for i in range(4)
    ]

    krb[:, 32:, :] = jnp.zeros((2, 96, 128), BF16)
    vrb[:, 32:, :] = jnp.zeros((2, 96, 128), BF16)
    for j in range(2):
        krb[j, pl.ds(pl.multiple_of(c * 16, 16), 16), :] = small[2 * c + j, 32:48, :]
        vrb[j, pl.ds(pl.multiple_of(c * 16, 16), 16), :] = small[2 * c + j, 48:64, :]
        qbuf[z, j, pl.ds(pl.multiple_of((x * 2 + c) * 32, 32), 32), :] = small[2 * c + j, 0:32, :]

    pl.semaphore_wait(barrier, 31)

    resp_rows = pl.ds(pl.multiple_of(c * 16, 16), 16)
    q_rows = pl.ds(pl.multiple_of((x * 2 + c) * 32, 32), 32)

    def send_plane(u):
        tz = lax.rem(z + PLANE_ORDER[u], 4)

        def one(i, carry):
            tx = lax.rem(x + i // 2, 4)
            tc = lax.rem(c + i, 2)
            target = (tz * 4 + tx) * 2 + tc
            for j in range(2):
                send(
                    small.at[2 * tc + j, pl.ds(0, 32), :], qbuf.at[z, j, q_rows, :],
                    q_recv.at[PLANE_BACK[u]], target, 0,
                )
            return carry

        lax.fori_loop(1 if u == 0 else 0, 8, one, 0)

    send_plane(0)
    for j in range(2):
        send(small.at[2 * other + j, pl.ds(32, 16), :], krb.at[j, resp_rows, :], small_recv.at[0], sibling, 1)
        send(small.at[2 * other + j, pl.ds(48, 16), :], vrb.at[j, resp_rows, :], small_recv.at[0], sibling, 1)
    send(prompt_keys.at[:, other_cols], kbuf.at[c], kv_recv.at[0], sibling, 2)
    send(prompt_values.at[:, other_cols], vbuf.at[c], kv_recv.at[1], sibling, 2)
    send_plane(2)
    send_plane(1)
    send_plane(3)
    send(out_weight.at[other_half, :], wbuf.at[:, w_lane], w_recv.at[0], sibling, 3)
    for copy in vocab_copies:
        copy.start()

    live = length[0]
    key_column = lax.broadcasted_iota(jnp.int32, (256, 128), 1)
    key_id = chip * 8 + (key_column // 16) * 4 + key_column % 16
    key_ok = (key_column < 32) & (key_column % 16 < 4) & (key_id < live)
    row_in_plane = lax.broadcasted_iota(jnp.int32, (256, 128), 0) // 8

    for u in range(4):
        t = lax.rem(z + PLANE_ORDER[u], 4)
        drain(qbuf.at[0, :, pl.ds(0, 224 if u == 0 else 256), :], q_recv.at[u])
        if u == 0:
            drain(krb.at[:, pl.ds(0, 32), :], small_recv.at[0])
            own_copies[0].wait()
            drain(kbuf.at[0], kv_recv.at[0])
        visible = key_ok & (key_id <= t * 32 + row_in_plane)
        for j in range(2):
            cols = slice(j * 128, (j + 1) * 128)
            q = qbuf[t, j]
            s0 = dot_nt(q, kbuf[0, :, cols])
            s1 = dot_nt(q, kbuf[1, :, cols])
            sr = jnp.where(visible, dot_nt(q, krb[j]), -jnp.inf)
            peak = jnp.maximum(
                jnp.maximum(jnp.max(s0, 1, keepdims=True), jnp.max(s1, 1, keepdims=True)),
                jnp.max(sr, 1, keepdims=True),
            ) * SCORE_SCALE
            p0 = jnp.exp2(s0 * SCORE_SCALE - peak)
            p1 = jnp.exp2(s1 * SCORE_SCALE - peak)
            pr = jnp.exp2(sr * SCORE_SCALE - peak)
            total = (
                jnp.sum(p0, 1, keepdims=True) + jnp.sum(p1, 1, keepdims=True)
                + jnp.sum(pr, 1, keepdims=True)
            )
            if u == 0 and j == 0:
                own_copies[1].wait()
                drain(vbuf.at[0], kv_recv.at[1])
            o = (
                dot_nn(p0.astype(BF16), vbuf[0, :, cols])
                + dot_nn(p1.astype(BF16), vbuf[1, :, cols])
                + dot_nn(pr.astype(BF16), vrb[j])
            )
            ostage[u, j] = o.astype(BF16)
            for half in range(2):
                rows = slice(half * 128, (half + 1) * 128)
                sstage[u, j, half, 0:1, :] = to_row(peak[rows])
                sstage[u, j, half, 1:2, :] = to_row(total[rows])
                owner = (t * 4 + 2 * half + j) * 2 + c
                part = ostage.at[u, j, pl.ds(half * 128, 128), :]
                stat = sstage.at[u, j, half]

                def to_other():
                    send(part, rbuf.at[chip], r_recv.at[0], owner, 4)
                    send(stat, rstat.at[chip], r_recv.at[1], owner, 5)

                def to_self():
                    pltpu.make_async_copy(part, rbuf.at[chip], own_sem.at[0]).start()
                    pltpu.make_async_copy(stat, rstat.at[chip], own_sem.at[1]).start()

                if u == 0:
                    pl.when(owner != me)(to_other)
                    pl.when(owner == me)(to_self)
                else:
                    to_other()

    drain(rstat.at[pl.ds(0, 15)], r_recv.at[1])
    drain(rstat.at[0], own_sem.at[1])
    peaks = rstat[:, 0, :]
    weight = jnp.exp2(peaks - jnp.max(peaks, 0, keepdims=True))
    weight = weight / jnp.sum(weight * rstat[:, 1, :], 0, keepdims=True)
    weight = jnp.concatenate([weight, jnp.zeros((112, 128), F32)], 0).T
    drain(rbuf.at[pl.ds(0, 15)], r_recv.at[0])
    drain(rbuf.at[0], own_sem.at[0])
    merged = weight[:, 0:1] * rbuf[0].astype(F32)
    for k in range(1, 16):
        merged += weight[:, k : k + 1] * rbuf[k].astype(F32)
    mrg[...] = merged
    block = jnp.concatenate([mrg[pl.ds(h, 16, stride=8), :] for h in range(8)], 1)
    head_group, row_group = lax.rem(x, 2), z * 2 + x // 2
    abuf[head_group, row_group] = block.astype(BF16)

    def spread_attn(i, carry):
        target = rel_chip(i // 4, i % 4) * 2 + c
        mine = abuf.at[head_group, row_group]
        send(mine, mine, a_recv.at[0], target, 6)
        return carry

    lax.fori_loop(1, 16, spread_attn, 0)
    own_copies[2].wait()
    drain(wbuf.at[:, pl.ds(0, 128)], w_recv.at[0])
    drain(rbuf.at[pl.ds(0, 15)], a_recv.at[0])
    projected = dot_nn(abuf[0].reshape(128, 1024), wbuf[pl.ds(0, 1024), :]) + dot_nn(
        abuf[1].reshape(128, 1024), wbuf[pl.ds(1024, 1024), :]
    )
    pown[0] = projected[:, :128]
    pown[1] = projected[:, 128:]
    send(pown.at[other], ppart, p_recv.at[0], sibling, 7)
    base = residual[...].astype(F32) + pown[c]
    drain(ppart, p_recv.at[0])
    layer = (base + ppart[...]).astype(BF16)
    layer_out[...] = layer
    layer = layer.astype(F32)
    gbuf[chip, c] = (layer * gain[...]).astype(BF16)
    ssbuf[me] = to_row(jnp.sum(layer * layer, 1, keepdims=True))

    def spread_features(i, carry):
        target = rel_chip(i // 4, i % 4) * 2 + c
        mine = gbuf.at[chip, c]
        send(mine, mine, g_recv.at[i], target, 8)
        return carry

    lax.fori_loop(1, 16, spread_features, 0)
    send(gbuf.at[chip, c], gbuf.at[chip, c], h_recv.at[0], sibling, 9)

    def spread_squares(i, carry):
        mine = ssbuf.at[me]
        send(mine, mine, s_recv.at[0], lax.rem(me + i, 32), 10)
        return carry

    lax.fori_loop(1, 32, spread_squares, 0)

    for copy in vocab_copies:
        copy.wait()
    acc[...] = jnp.zeros_like(acc)

    def logits_of(i):
        source = lax.rem(z + 4 - i // 4, 4) * 4 + lax.rem(x + 4 - i % 4, 4)
        return source

    def step(i, carry):
        source = logits_of(i)

        @pl.when(i < 16)
        def _():
            @pl.when(i > 0)
            def _():
                drain(gbuf.at[0, 0], g_recv.at[i])
                block = gbuf.at[source, c]
                send(block, block, h_recv.at[i], sibling, 9)

        @pl.when(i > 0)
        def _():
            prev = logits_of(i - 1)
            drain(gbuf.at[0, 0], h_recv.at[i - 1])
            features = jnp.concatenate([gbuf[prev, 0], gbuf[prev, 1]], 1)
            acc[...] += dot_nn(features, wv[pl.ds(pl.multiple_of(prev * 256, 256), 256), :])

        return carry

    lax.fori_loop(0, 17, step, 0)

    drain(ssbuf.at[pl.ds(0, 31)], s_recv.at[0])
    squares = jnp.sum(ssbuf[:, 0, :], 0, keepdims=True)
    inverse = to_column(lax.rsqrt(squares / D + 1e-06))
    logits = acc[...] * inverse
    top = jnp.max(logits, 1, keepdims=True)
    exp_total = jnp.sum(jnp.exp(logits - top), 1, keepdims=True)
    target = to_column(targets[...].astype(F32)).astype(jnp.int32) - me * VOCAB_DEV
    hit = lax.broadcasted_iota(jnp.int32, (ROWS, VOCAB_DEV), 1) == target
    target_logit = jnp.sum(jnp.where(hit, logits, 0.0), 1, keepdims=True)
    fbuf[me, 0:1, :] = to_row(top)
    fbuf[me, 1:2, :] = to_row(exp_total)
    fbuf[me, 2:3, :] = to_row(target_logit)

    def spread_totals(i, carry):
        mine = fbuf.at[me]
        send(mine, mine, f_recv.at[0], lax.rem(me + i, 32), 11)
        return carry

    lax.fori_loop(1, 32, spread_totals, 0)
    drain(fbuf.at[pl.ds(0, 31)], f_recv.at[0])
    tops = fbuf[:, 0, :]
    top = jnp.max(tops, 0, keepdims=True)
    whole = jnp.sum(fbuf[:, 1, :] * jnp.exp(tops - top), 0, keepdims=True)
    loss = top + jnp.log(whole) - jnp.sum(fbuf[:, 2, :], 0, keepdims=True)
    row_ids = lax.broadcasted_iota(jnp.int32, (1, ROWS), 1)
    row_loss[...] = jnp.where(row_ids < live, loss, 0.0)

    drain(kbuf.at[0, pl.ds(0, 992), :], send_sem.at[0])
    drain(krb.at[:, pl.ds(0, 32), :], send_sem.at[1])
    drain(kbuf, send_sem.at[2])
    drain(wbuf.at[:, pl.ds(0, 128)], send_sem.at[3])
    owns = 1
    drain(rbuf.at[pl.ds(0, 16 - owns)], send_sem.at[4])
    drain(rstat.at[pl.ds(0, 16 - owns)], send_sem.at[5])
    drain(rbuf.at[pl.ds(0, 15)], send_sem.at[6])
    drain(ppart, send_sem.at[7])
    drain(rbuf.at[pl.ds(0, 15)], send_sem.at[8])
    drain(rbuf, send_sem.at[9])
    drain(ssbuf.at[pl.ds(0, 31)], send_sem.at[10])
    drain(fbuf.at[pl.ds(0, 31)], send_sem.at[11])


def local(
    queries, prompt_keys, prompt_values, response_keys, response_values, resp_len, residual,
    out_weight, norm_gain, vocab_weight, targets,
):
    rows = queries.shape[0]

    def by_key_head(a):
        return a.reshape(rows, KEY_VALUE_HEADS, -1, HEAD_SIZE).transpose(1, 0, 2, 3).reshape(
            KEY_VALUE_HEADS, -1, HEAD_SIZE
        )

    pad = ((0, 0), (0, 16 - rows), (0, 0))
    small = jnp.concatenate(
        [
            by_key_head(queries),
            jnp.pad(by_key_head(response_keys), pad),
            jnp.pad(by_key_head(response_values), pad),
        ],
        1,
    )
    vmem = pl.BlockSpec(memory_space=pltpu.VMEM)
    hbm = pl.BlockSpec(memory_space=pl.ANY)
    dma = pltpu.SemaphoreType.DMA
    layer_out, row_loss = pl.pallas_call(
        kernel,
        out_shape=(
            jax.ShapeDtypeStruct((ROWS, 128), BF16),
            jax.ShapeDtypeStruct((1, ROWS), F32),
        ),
        in_specs=[vmem, hbm, hbm, pl.BlockSpec(memory_space=pltpu.SMEM), vmem, hbm, vmem, hbm, vmem],
        out_specs=(vmem, vmem),
        scratch_shapes=[
            pltpu.VMEM((2, KEYS_DEV, 256), BF16),
            pltpu.VMEM((2, KEYS_DEV, 256), BF16),
            pltpu.VMEM((2, 128, 128), BF16),
            pltpu.VMEM((2, 128, 128), BF16),
            pltpu.VMEM((4, 2, 256, 128), BF16),
            pltpu.VMEM((4, 2, 256, 128), BF16),
            pltpu.VMEM((4, 2, 2, 8, 128), F32),
            pltpu.VMEM((16, 128, 128), BF16),
            pltpu.VMEM((16, 8, 128), F32),
            pltpu.VMEM((128, 128), F32),
            pltpu.VMEM((2, 8, 16, 1024), BF16),
            pltpu.VMEM((2048, 256), BF16),
            pltpu.VMEM((2, 128, 128), F32),
            pltpu.VMEM((128, 128), F32),
            pltpu.VMEM((16, 2, 128, 128), BF16),
            pltpu.VMEM((32, 1, 128), F32),
            pltpu.VMEM((D, VOCAB_DEV), BF16),
            pltpu.VMEM((ROWS, VOCAB_DEV), F32),
            pltpu.VMEM((32, 8, 128), F32),
            dma((3,)),
            dma((4,)),
            dma((2,)),
            dma((1,)),
            dma((1,)),
            dma((4,)),
            dma((2,)),
            dma((2,)),
            dma((1,)),
            dma((1,)),
            dma((16,)),
            dma((16,)),
            dma((1,)),
            dma((1,)),
            dma((12,)),
        ],
        compiler_params=pltpu.CompilerParams(
            collective_id=0, has_side_effects=True, vmem_limit_bytes=56 * 1024 * 1024
        ),
        name="score_response",
    )(
        small, prompt_keys, prompt_values, resp_len, residual, out_weight,
        norm_gain.reshape(1, 128), vocab_weight, targets.reshape(1, ROWS),
    )
    return layer_out, row_loss.reshape(ROWS)


def solution(mesh):
    placed = (
        P(("batch", "seq"), None),
        P(("batch", "seq"), None),
        P(("batch", "seq"), None),
        P(("batch", "seq"), None),
        P(("batch", "seq"), None),
        P("batch"),
        P("batch", "seq"),
        P(None, "seq"),
        P("seq"),
        P(None, "seq"),
        P("batch"),
    )
    return jax.shard_map(
        local,
        mesh=mesh,
        in_specs=placed,
        out_specs=(P("batch", "seq"), P("batch")),
        check_vma=False,
    )
```

time: 692 us -> 68.5 us (0.10)
  blocking collectives: 237 us -> 0 us
  waiting for transfers between devices: 237 us -> 0 us
  other arithmetic: 125 us -> 1.33 us
  Pallas kernels: 0 us -> 62.2 us
  local copies, waits for them, and re-layouts: 49.5 us -> 3.33 us
  matrix products: 20.9 us -> 0 us
  between operations: 14.6 us -> 1.29 us
    all_gather x3 -> x0, waiting for transfers between devices: 237 us -> none  [the longest x1 153 us: merged(): gathered = jax.tree.map(lambda a: lax.all_gather(a, axis), part)]
    psum x2 -> x0, blocking collectives: 128 us -> none  [the longest x1 65.2 us: local(): whole_total, target_logit = lax.psum((exp_total, target_part), 'seq')]
    add x64 -> x0, other arithmetic: 119 us -> none  [the longest x31 117 us: join_partials(): output = output_a * scale_a[..., None] + output_b * scale_b[..., None]]
    pmax x1 -> x0, blocking collectives: 62.3 us -> none  [local(): top_logit = lax.pmax(local_peak, 'seq')]
    pallas_call x0 -> x1, Pallas kernels: none -> 62.2 us  [local(): pl.pallas_call(kernel, out_shape=(jax.ShapeDtypeStruct((ROWS, 128), BF16)...]
    all_gather x2 -> x0, blocking collectives: 47.4 us -> none  [merged(): gathered = jax.tree.map(lambda a: lax.all_gather(a, axis), part)]
    dynamic_slice x97 -> x0, local copies, waits for them, and re-layouts: 32.9 us -> none  [the longest x93 29 us: take(): lax.dynamic_index_in_dim(a, source, 0, False)]
    dot_general x10 -> x0, matrix products: 20.9 us -> none  [the longest x1 10 us: local(): jnp.dot(lax.all_gather(normed, 'seq', axis=1, tiled=True), vocab_weight,...]
  transfers between devices with their start and end apart: 3 -> 0, of which waited for: 3 -> 0; matrix products, arithmetic and copies ran while one was open for 1% -> 0% of each run, Pallas kernels for 0% -> 0%
where the time goes in v1:
time: 68.5 us; the launch traced here: 68.2 us
  Pallas kernels  62.2 us (91%)
  local copies, waits for them, and re-layouts  3.33 us (5%)
  other arithmetic  1.33 us (2%)
  between operations  1.29 us (2%)
    pallas_call x1, Pallas kernels, local(): pl.pallas_call(kernel, out_shape=(jax.ShapeDtypeStruct((ROWS, 128), BF16)...  62.2 us
    unnamed x2, local copies, waits for them, and re-layouts  2.57 us

profile of v1, /device:TPU:1, one launch (start us, length us, event | category | flops | bytes accessed | tf_op | source)
XLA Modules:
  0.0 68.2 jit_solution(2696921367378956814)
XLA Ops:
  1.3 0.8 %copy_bitcast_fusion.1 = bf16[4,32,128]{2,1,0:T(8,128)(2,1)S(1)} fusion(bf16[1,4,32,128]{3,1,2,0:T(4,128)(2,1)} %bitcast.22), kind=kLoop, calls=%fused_computation.9 | loop fusion | bytes 65536 | tf_op jit(solution)/shard_map/reshape | solution.py:343
  2.0 1.3 %fusion.4.small = bf16[4,64,128]{2,1,0:T(8,128)(2,1)} fusion(bf16[4,4,128]{2,1,0:T(4,128)(2,1)} %bitcast.23, bf16[4,4,128]{2,1,0:T(4,128)(2,1)} %bitcast.24, bf16[4,32,128]{2,1,0:T(8,128)(2,1)S(1)} %copy_bitcast_fusion.1), kind=kLoop, calls=%fused_computation.7 | loop fusion | flops 393216 | bytes 106496 | tf_op jit(solution)/shard_map/concatenate | solution.py:348
  3.4 62.2 %score_response.1 = (bf16[128,128]{1,0:T(8,128)(2,1)}, f32[1,128]{1,0:T(1,128)}) custom-call(bf16[4,64,128]{2,1,0:T(8,128)(2,1)} %fusion.4.small, bf16[1024,512]{1,0:T(8,128)(2,1)} %prompt_keys.1, bf16[1024,512]{1,0:T(8,128)(2,1)} %prompt_values.1, s32[1]{0:T(128)S(6)} %copy.20.length, bf16[128,128]{1,0:T(8,128)(2,1)} %residual.1, ...), custom_call_target="tpu_custom_call" | custom-call | tf_op jit(solution)/shard_map/score_response/pallas_call | solution.py:359
  65.6 1.4 %copy.21 = bf16[128,128]{1,0:T(8,128)(2,1)} copy(bf16[128,128]{1,0:T(8,128)(2,1)} %get-tuple-element.8) | data formatting | bytes 65536
  67.0 1.2 %copy.22 = f32[128]{0:T(128)} copy(f32[128]{0:T(128)} %bitcast.27) | data formatting | bytes 1024

commit v2 on v1

v2 whole, which is shorter than its diff:
```python
import functools

import jax
import jax.numpy as jnp
from jax import lax
from jax.experimental import pallas as pl
from jax.experimental.pallas import tpu as pltpu
from jax.sharding import PartitionSpec as P

D = 4096
KEY_VALUE_HEADS = 4
HEAD_SIZE = 128
ROWS = 128
VOCAB_DEV = 2432
KEYS_DEV = 1024
LOG2E = 1.4426950408889634
SCORE_SCALE = LOG2E * HEAD_SIZE ** (-0.5)
MESH = pl.DeviceIdType.MESH
F32 = jnp.float32
BF16 = jnp.bfloat16


def dot_nt(a, b):
    return lax.dot_general(a, b, (((1,), (1,)), ((), ())), preferred_element_type=F32)


def dot_nn(a, b):
    return jnp.dot(a, b, preferred_element_type=F32)


def eye_mask():
    return lax.broadcasted_iota(jnp.int32, (128, 128), 0) == lax.broadcasted_iota(
        jnp.int32, (128, 128), 1
    )


def to_row(column):
    return jnp.sum(jnp.where(eye_mask(), column, 0.0), axis=0, keepdims=True)


def to_column(row):
    return jnp.sum(jnp.where(eye_mask(), row, 0.0), axis=1, keepdims=True)


def drain(ref, sem):
    pltpu.make_async_copy(ref, ref, sem).wait()


def kernel(
    queries, response_keys, response_values, prompt_keys, prompt_values, length, residual_in,
    out_weight, gain_in, vocab_weight, targets_in,
    layer_out, row_loss,
    residual, gain, targets, spread, small, resp, respbuf, kbuf, vbuf, qbuf, ostage, sstage, rbuf, rstat, mrg, abuf, wbuf,
    pown, ppart, gbuf, ssbuf, ssplane, wv, acc, fbuf,
    local_sem, vocab_sem, kv_recv, w_recv, small_recv, q_ring, q_diag, r_recv, own_sem, a_recv,
    p_recv, g_ring, g_diag, h_recv, s_recv, f_recv, send_sem,
):
    me = lax.axis_index("seq")
    z, x, c = me // 8, (me // 2) % 4, me % 2
    chip = me // 2
    other = 1 - c
    sibling = chip * 2 + other

    def turn(a, d):
        return lax.rem(a + d, 4)

    def device(cz, cx, core):
        return (cz * 4 + cx) * 2 + core

    def send(src, dst, sem, target, kind):
        pltpu.make_async_remote_copy(
            src_ref=src, dst_ref=dst, send_sem=send_sem.at[kind], recv_sem=sem,
            device_id={"seq": target}, device_id_type=MESH,
        ).start()

    my_cols = pl.ds(pl.multiple_of(c * 256, 256), 256)
    other_cols = pl.ds(pl.multiple_of(other * 256, 256), 256)
    my_half = pl.ds(pl.multiple_of(c * 2048, 2048), 2048)
    other_half = pl.ds(pl.multiple_of(other * 2048, 2048), 2048)
    w_lane = pl.ds(pl.multiple_of(c * 128, 128), 128)

    barrier = pltpu.get_barrier_semaphore()
    x_peers = [device(z, turn(x, d), core) for d in (2, 1, 3) for core in (c, other)]
    z_peers = [device(turn(z, d), x, core) for d in (2, 1, 3) for core in (c, other)]
    for peer in z_peers + x_peers + [sibling]:
        pl.semaphore_signal(barrier, inc=1, device_id={"seq": peer}, device_id_type=MESH)

    own_copies = [
        pltpu.make_async_copy(prompt_keys.at[:, my_cols], kbuf.at[c], local_sem.at[0]),
        pltpu.make_async_copy(prompt_values.at[:, my_cols], vbuf.at[c], local_sem.at[1]),
        pltpu.make_async_copy(out_weight.at[my_half, :], wbuf.at[:, w_lane], local_sem.at[2]),
        pltpu.make_async_copy(residual_in, residual, local_sem.at[3]),
        pltpu.make_async_copy(gain_in, gain, local_sem.at[4]),
        pltpu.make_async_copy(targets_in, targets, local_sem.at[5]),
    ]
    for copy in own_copies:
        copy.start()
    vocab_copies = [
        pltpu.make_async_copy(
            vocab_weight.at[pl.ds(i * 1024, 1024), :], wv.at[pl.ds(i * 1024, 1024), :],
            vocab_sem.at[i],
        )
        for i in range(4)
    ]

    wide = queries[...].astype(F32)
    for head in range(32):
        spread[head // 8, pl.ds(head % 8, 4, stride=8), :] = wide[:, head * 128 : head * 128 + 128]
    nothing = jnp.zeros((12, 128), F32)
    for g in range(4):
        cols = slice(g * 128, g * 128 + 128)
        small[g] = spread[g].astype(BF16)
        resp[g, 0:16, :] = jnp.concatenate([response_keys[:, cols].astype(F32), nothing], 0).astype(BF16)
        resp[g, 16:32, :] = jnp.concatenate([response_values[:, cols].astype(F32), nothing], 0).astype(BF16)
    q_rows = pl.ds(pl.multiple_of((x * 2 + c) * 32, 32), 32)
    my_heads, other_heads = pl.ds(2 * c, 2), pl.ds(2 * other, 2)
    for j in range(2):
        qbuf[z, j, q_rows, :] = small[2 * c + j]
        respbuf[c, j] = resp[2 * c + j]

    pl.semaphore_wait(barrier, 13)

    send(resp.at[other_heads], respbuf.at[c], small_recv.at[0], sibling, 1)
    def q_half(cz, cx, part):
        return qbuf.at[cz, part, pl.ds(pl.multiple_of(cx * 64, 64), 64), :]

    mine = qbuf.at[z, :, q_rows, :]
    send(small.at[other_heads], mine, q_ring.at[0, 0], sibling, 0)
    for d in (1, 3, 2):
        for core in (c, other):
            heads = small.at[pl.ds(2 * core, 2)]
            send(heads, mine, q_ring.at[0, 4 - d], device(z, turn(x, d), core), 0)
            send(heads, mine, q_ring.at[1, 4 - d], device(turn(z, d), x, core), 0)
    send(prompt_keys.at[:, other_cols], kbuf.at[c], kv_recv.at[0], sibling, 2)
    send(prompt_values.at[:, other_cols], vbuf.at[c], kv_recv.at[1], sibling, 2)
    for d in (1, 3, 2):
        sx, sz = turn(x, d), turn(z, d)
        drain(qbuf.at[0, 0, pl.ds(0, 128), :], q_ring.at[0, d])
        for e in (1, 3, 2):
            block = q_half(z, sx, 0)
            send(block, block, q_diag.at[0, (4 - e) * 4 + d], device(turn(z, e), x, c), 12)
        drain(qbuf.at[0, 0, pl.ds(0, 128), :], q_ring.at[1, d])
        for e in (1, 3, 2):
            block = q_half(sz, x, 1)
            send(block, block, q_diag.at[1, d * 4 + 4 - e], device(z, turn(x, e), c), 12)
    drain(qbuf.at[0, 0, pl.ds(0, 64), :], q_ring.at[0, 0])
    send(out_weight.at[other_half, :], wbuf.at[:, w_lane], w_recv.at[0], sibling, 3)
    for copy in vocab_copies:
        copy.start()

    live = length[0]
    key_column = lax.broadcasted_iota(jnp.int32, (256, 32), 1)
    key_id = chip * 8 + (key_column // 16) * 4 + key_column % 16
    key_ok = (key_column % 16 < 4) & (key_id < live)
    row_in_plane = lax.broadcasted_iota(jnp.int32, (256, 32), 0) // 8
    drain(resp.at[pl.ds(0, 2)], small_recv.at[0])
    own_copies[0].wait()
    drain(kbuf.at[0], kv_recv.at[0])
    own_copies[1].wait()
    drain(vbuf.at[0], kv_recv.at[1])

    def with_ones(v):
        return jnp.concatenate([v, jnp.ones_like(v)], 1)

    for u, offset in enumerate((0, 1 + 2 * (x % 2), 2, 3 - 2 * (x % 2))):
        t = turn(z, offset)
        if u > 0:
            for dx in (1, 3, 2):
                for part in range(2):
                    drain(qbuf.at[0, 0, pl.ds(0, 64), :], q_diag.at[part, offset * 4 + dx])

        visible = key_ok & (key_id <= t * 32 + row_in_plane)
        for j in range(2):
            cols = slice(j * 128, (j + 1) * 128)
            q = qbuf[t, j]
            s0 = dot_nt(q, kbuf[0, :, cols])
            s1 = dot_nt(q, kbuf[1, :, cols])
            resp_keys = jnp.concatenate([respbuf[0, j, 0:16, :], respbuf[1, j, 0:16, :]], 0)
            resp_values = jnp.concatenate([respbuf[0, j, 16:32, :], respbuf[1, j, 16:32, :]], 0)
            sr = jnp.where(visible, dot_nt(q, resp_keys), -jnp.inf)
            peak = jnp.maximum(
                jnp.maximum(jnp.max(s0, 1, keepdims=True), jnp.max(s1, 1, keepdims=True)),
                jnp.max(sr, 1, keepdims=True),
            ) * SCORE_SCALE
            p0 = jnp.exp2(s0 * SCORE_SCALE - peak)
            p1 = jnp.exp2(s1 * SCORE_SCALE - peak)
            pr = jnp.exp2(sr * SCORE_SCALE - peak)
            o = (
                dot_nn(p0.astype(BF16), with_ones(vbuf[0, :, cols]))
                + dot_nn(p1.astype(BF16), with_ones(vbuf[1, :, cols]))
                + dot_nn(pr.astype(BF16), with_ones(resp_values))
            )
            total = o[:, 128:]
            ostage[u, j] = o[:, :128].astype(BF16)
            for half in range(2):
                rows = slice(half * 128, (half + 1) * 128)
                sstage[u, j, half, 0:1, :] = to_row(peak[rows])
                sstage[u, j, half, 1:2, :] = to_row(total[rows])
                quarter = 2 * half + j
                owner = device(t, quarter, c)
                part = ostage.at[u, j, pl.ds(half * 128, 128), :]
                stat = sstage.at[u, j, half]

                def to_owner():
                    send(part, rbuf.at[chip], r_recv.at[0], owner, 4)
                    send(stat, rstat.at[chip], r_recv.at[1], owner, 5)

                if u > 0:
                    to_owner()
                    continue
                pl.when(owner != me)(to_owner)

                @pl.when(owner == me)
                def _():
                    pltpu.make_async_copy(part, rbuf.at[chip], own_sem.at[0]).start()
                    pltpu.make_async_copy(stat, rstat.at[chip], own_sem.at[1]).start()

    drain(rstat.at[pl.ds(0, 15)], r_recv.at[1])
    drain(rstat.at[0], own_sem.at[1])
    peaks = rstat[:, 0, :]
    weight = jnp.exp2(peaks - jnp.max(peaks, 0, keepdims=True))
    weight = weight / jnp.sum(weight * rstat[:, 1, :], 0, keepdims=True)
    weight = jnp.concatenate([weight, jnp.zeros((112, 128), F32)], 0).T
    drain(rbuf.at[pl.ds(0, 15)], r_recv.at[0])
    drain(rbuf.at[0], own_sem.at[0])
    merged = weight[:, 0:1] * rbuf[0].astype(F32)
    for k in range(1, 16):
        merged += weight[:, k : k + 1] * rbuf[k].astype(F32)
    mrg[...] = merged
    block = jnp.concatenate([mrg[pl.ds(h, 16, stride=8), :] for h in range(8)], 1)
    abuf[z, x] = block.astype(BF16)

    def torus_distance(d):
        return min(d[0], 4 - d[0]) + min(d[1], 4 - d[1])

    far_first = sorted([(dz, dx) for dz in range(4) for dx in range(4)], key=lambda d: -torus_distance(d))
    for dz, dx in far_first[:-1]:
        send(abuf.at[z, x], abuf.at[z, x], a_recv.at[0], device(turn(z, dz), turn(x, dx), c), 6)
    for copy in own_copies[2:]:
        copy.wait()
    drain(wbuf.at[:, pl.ds(0, 128)], w_recv.at[0])
    drain(rbuf.at[pl.ds(0, 15)], a_recv.at[0])
    projected = None
    for j in range(2):
        attn = jnp.concatenate(
            [abuf[t, 2 * half + j] for t in range(4) for half in range(2)], 0
        )
        term = dot_nn(attn, wbuf[pl.ds(j * 1024, 1024), :])
        projected = term if j == 0 else projected + term
    pown[0] = projected[:, :128]
    pown[1] = projected[:, 128:]
    send(pown.at[other], ppart, p_recv.at[0], sibling, 7)
    base = residual[...].astype(F32) + pown[c]
    drain(ppart, p_recv.at[0])
    layer = (base + ppart[...]).astype(BF16)
    layer_out[...] = layer
    layer = layer.astype(F32)
    gbuf[z, x, c] = (layer * gain[...]).astype(BF16)
    ssbuf[x * 2 + c] = to_row(jnp.sum(layer * layer, 1, keepdims=True))

    def gather(full, half, ring, diag, kind, on_ring):
        for d in (1, 3, 2):
            send(full(z, x), full(z, x), ring.at[0, 4 - d], device(z, turn(x, d), c), kind)
            send(full(z, x), full(z, x), ring.at[1, 4 - d], device(turn(z, d), x, c), kind)
        for d in (1, 3, 2):
            sx, sz = turn(x, d), turn(z, d)
            drain(full(0, 0), ring.at[0, d])
            for e in (1, 3, 2):
                block = half(z, sx, 0)
                send(block, block, diag.at[0, (4 - e) * 4 + d], device(turn(z, e), x, c), kind)
            on_ring(z, sx, d)
            drain(full(0, 0), ring.at[1, d])
            for e in (1, 3, 2):
                block = half(sz, x, 1)
                send(block, block, diag.at[1, d * 4 + 4 - e], device(z, turn(x, e), c), kind)
            on_ring(sz, x, d * 4)

    def g_full(cz, cx):
        return gbuf.at[cz, cx, c]

    def g_half(cz, cx, part):
        return gbuf.at[cz, cx, c, pl.ds(part * 64, 64), :]

    def to_sibling(cz, cx, index):
        send(g_full(cz, cx), g_full(cz, cx), h_recv.at[index], sibling, 9)

    to_sibling(z, x, 0)
    for peer in x_peers + [sibling]:
        mine = ssbuf.at[x * 2 + c]
        send(mine, mine, s_recv.at[0], peer, 10)
    gather(g_full, g_half, g_ring, g_diag, 8, to_sibling)
    drain(ssbuf.at[pl.ds(0, 7)], s_recv.at[0])
    ssplane[z] = jnp.sum(ssbuf[:, 0, :], 0, keepdims=True)
    for d in (2, 1, 3):
        send(ssplane.at[z], ssplane.at[z], s_recv.at[1], device(turn(z, d), x, c), 11)

    def plane_features(cz):
        return jnp.concatenate([gbuf[cz, cx, core] for cx in range(4) for core in range(2)], 1)

    def plane_rows(cz):
        return pl.ds(pl.multiple_of(cz * 1024, 1024), 1024)

    for copy in vocab_copies:
        copy.wait()
    for dx in range(4):
        drain(gbuf.at[0, 0, 0], h_recv.at[dx])
    acc[...] = dot_nn(plane_features(z), wv[plane_rows(z), :])
    for dz in (1, 3, 2):
        for dx in (1, 3, 2):
            for part in range(2):
                drain(g_half(0, 0, part), g_diag.at[part, dz * 4 + dx])
            to_sibling(turn(z, dz), turn(x, dx), dz * 4 + dx)
    for dz in (1, 3, 2):
        for dx in range(4):
            drain(gbuf.at[0, 0, 0], h_recv.at[dz * 4 + dx])
    planes = [turn(z, dz) for dz in (1, 2, 3)]
    features = [plane_features(cz) for cz in planes]
    for n in range(0, VOCAB_DEV, 512):
        cols = slice(n, min(n + 512, VOCAB_DEV))
        part = acc[:, cols]
        for cz, f in zip(planes, features):
            part += dot_nn(f, wv[plane_rows(cz), cols])
        acc[:, cols] = part

    drain(ssplane.at[pl.ds(0, 3)], s_recv.at[1])
    squares = jnp.sum(ssplane[:, 0, :], 0, keepdims=True)
    inverse = to_column(lax.rsqrt(squares / D + 1e-06))
    logits = acc[...] * inverse
    top = jnp.max(logits, 1, keepdims=True)
    exp_total = jnp.sum(jnp.exp(logits - top), 1, keepdims=True)
    target = to_column(targets[...].astype(F32)).astype(jnp.int32) - me * VOCAB_DEV
    hit = lax.broadcasted_iota(jnp.int32, (ROWS, VOCAB_DEV), 1) == target
    target_logit = jnp.sum(jnp.where(hit, logits, 0.0), 1, keepdims=True)
    fbuf[me] = jnp.concatenate([to_row(top), to_row(exp_total), to_row(target_logit)], 1)

    for dz, dx in far_first:
        for core in (c, other):
            if (dz, dx) != (0, 0) or core is other:
                target_device = device(turn(z, dz), turn(x, dx), core)
                send(fbuf.at[me], fbuf.at[me], f_recv.at[0], target_device, 13)
    drain(fbuf.at[pl.ds(0, 31)], f_recv.at[0])
    tops = fbuf[:, 0, 0:128]
    top = jnp.max(tops, 0, keepdims=True)
    whole = jnp.sum(fbuf[:, 0, 128:256] * jnp.exp(tops - top), 0, keepdims=True)
    loss = top + jnp.log(whole) - jnp.sum(fbuf[:, 0, 256:384], 0, keepdims=True)
    row_ids = lax.broadcasted_iota(jnp.int32, (1, ROWS), 1)
    row_loss[...] = jnp.where(row_ids < live, loss, 0.0)

    drain(kbuf.at[0, pl.ds(0, 416), :], send_sem.at[0])
    drain(resp.at[pl.ds(0, 2)], send_sem.at[1])
    drain(kbuf, send_sem.at[2])
    drain(wbuf.at[:, pl.ds(0, 128)], send_sem.at[3])
    drain(rbuf.at[pl.ds(0, 15)], send_sem.at[4])
    drain(rstat.at[pl.ds(0, 15)], send_sem.at[5])
    drain(rbuf.at[pl.ds(0, 15)], send_sem.at[6])
    drain(ppart, send_sem.at[7])
    drain(rbuf.at[pl.ds(0, 15)], send_sem.at[8])
    drain(rbuf, send_sem.at[9])
    drain(ssbuf.at[pl.ds(0, 7)], send_sem.at[10])
    drain(ssplane.at[pl.ds(0, 3)], send_sem.at[11])
    drain(kbuf.at[0, pl.ds(0, 576), :], send_sem.at[12])
    drain(fbuf.at[pl.ds(0, 31)], send_sem.at[13])


def hand_over(layer, loss, layer_out, loss_out):
    layer_out[...] = layer[...]
    loss_out[...] = loss[...]


def local(
    queries, prompt_keys, prompt_values, response_keys, response_values, resp_len, residual,
    out_weight, norm_gain, vocab_weight, targets,
):
    vmem = pl.BlockSpec(memory_space=pltpu.VMEM)
    hbm = pl.BlockSpec(memory_space=pl.ANY)
    dma = pltpu.SemaphoreType.DMA
    shapes = (
        jax.ShapeDtypeStruct((ROWS, 128), BF16),
        jax.ShapeDtypeStruct((1, ROWS), F32),
    )
    results = pl.pallas_call(
        kernel,
        out_shape=shapes,
        in_specs=[
            vmem, vmem, vmem, hbm, hbm, pl.BlockSpec(memory_space=pltpu.SMEM), hbm, hbm, hbm,
            hbm, hbm,
        ],
        out_specs=(vmem, vmem),
        scratch_shapes=[
            pltpu.VMEM((ROWS, 128), BF16),
            pltpu.VMEM((1, 128), F32),
            pltpu.VMEM((1, ROWS), jnp.int32),
            pltpu.VMEM((4, 32, 128), F32),
            pltpu.VMEM((4, 32, 128), BF16),
            pltpu.VMEM((4, 32, 128), BF16),
            pltpu.VMEM((2, 2, 32, 128), BF16),
            pltpu.VMEM((2, KEYS_DEV, 256), BF16),
            pltpu.VMEM((2, KEYS_DEV, 256), BF16),
            pltpu.VMEM((4, 2, 256, 128), BF16),
            pltpu.VMEM((4, 2, 256, 128), BF16),
            pltpu.VMEM((4, 2, 2, 8, 128), F32),
            pltpu.VMEM((16, 128, 128), BF16),
            pltpu.VMEM((16, 8, 128), F32),
            pltpu.VMEM((128, 128), F32),
            pltpu.VMEM((4, 4, 16, 1024), BF16),
            pltpu.VMEM((2048, 256), BF16),
            pltpu.VMEM((2, 128, 128), F32),
            pltpu.VMEM((128, 128), F32),
            pltpu.VMEM((4, 4, 2, 128, 128), BF16),
            pltpu.VMEM((8, 1, 128), F32),
            pltpu.VMEM((4, 1, 128), F32),
            pltpu.VMEM((D, VOCAB_DEV), BF16),
            pltpu.VMEM((ROWS, VOCAB_DEV), F32),
            pltpu.VMEM((32, 1, 384), F32),
            dma((6,)),
            dma((4,)),
            dma((2,)),
            dma((1,)),
            dma((1,)),
            dma((2, 4)),
            dma((2, 16)),
            dma((2,)),
            dma((2,)),
            dma((1,)),
            dma((1,)),
            dma((2, 4)),
            dma((2, 16)),
            dma((16,)),
            dma((2,)),
            dma((1,)),
            dma((14,)),
        ],
        compiler_params=pltpu.CompilerParams(
            collective_id=0, has_side_effects=True, vmem_limit_bytes=56 * 1024 * 1024
        ),
        name="score_response",
    )(
        queries, response_keys, response_values, prompt_keys, prompt_values, resp_len, residual,
        out_weight, norm_gain.reshape(1, 128), vocab_weight, targets.reshape(1, ROWS),
    )
    layer_out, row_loss = pl.pallas_call(
        hand_over, out_shape=shapes, in_specs=[vmem, vmem], out_specs=(vmem, vmem), name="hand_over"
    )(*results)
    return layer_out, row_loss.reshape(ROWS)


def solution(mesh):
    placed = (
        P(("batch", "seq"), None),
        P(("batch", "seq"), None),
        P(("batch", "seq"), None),
        P(("batch", "seq"), None),
        P(("batch", "seq"), None),
        P("batch"),
        P("batch", "seq"),
        P(None, "seq"),
        P("seq"),
        P(None, "seq"),
        P("batch"),
    )
    return jax.shard_map(
        local,
        mesh=mesh,
        in_specs=placed,
        out_specs=(P("batch", "seq"), P("batch")),
        check_vma=False,
    )
```

time: 68.5 us -> 59.7 us (0.87)
  Pallas kernels: 62.2 us -> 58.2 us
  local copies, waits for them, and re-layouts: 3.33 us -> 0 us
  other arithmetic: 1.33 us -> 0 us
    pallas_call x1 -> x2, Pallas kernels: 62.2 us -> 58.2 us  [the longest x1 56.8 us: local(): pl.pallas_call(kernel, out_shape=shapes, in_specs=[vmem, vmem, vmem, hbm,...]
    unnamed x2 -> x0, local copies, waits for them, and re-layouts: 2.57 us -> none
    concatenate x1 -> x0, other arithmetic: 1.33 us -> none  [local(): jnp.concatenate([by_key_head(queries), jnp.pad(by_key_head(response_keys)...]
    reshape x1 -> x0, local copies, waits for them, and re-layouts: 0.77 us -> none  [by_key_head(): a.reshape(rows, KEY_VALUE_HEADS, -1, HEAD_SIZE).transpose(1, 0, 2, 3)]
where the time goes in v2:
time: 59.7 us; the launch traced here: 59.5 us
  Pallas kernels  58.2 us (97%)
  between operations  1.29 us (2%)
    pallas_call x1, Pallas kernels, local(): pl.pallas_call(kernel, out_shape=shapes, in_specs=[vmem, vmem, vmem, hbm,...  56.8 us
    pallas_call x1, Pallas kernels, local(): pl.pallas_call(hand_over, out_shape=shapes, in_specs=[vmem, vmem], out_sp...  1.38 us

profile of v2, /device:TPU:1, one launch (start us, length us, event | category | flops | bytes accessed | tf_op | source)
XLA Modules:
  0.0 59.5 jit_solution(8972921450988512085)
XLA Ops:
  1.3 56.8 %score_response.1 = (bf16[128,128]{1,0:T(8,128)(2,1)}, f32[1,128]{1,0:T(1,128)}) custom-call(bf16[4,4096]{1,0:T(4,128)(2,1)} %queries.1, bf16[4,512]{1,0:T(4,128)(2,1)} %response_keys.1, bf16[4,512]{1,0:T(4,128)(2,1)} %response_values.1, bf16[1024,512]{1,0:T(8,128)(2,1)} %prompt_keys.1, bf16[1024,512]{1,0:T(8,128)(2,1)} %prompt_values.1, s32[1]{0:T(128)S(6)} %copy.13.length, ...), custom_call_target="tpu_custom_call" | custom-call | tf_op jit(solution)/shard_map/score_response/pallas_call | solution.py:381
  58.1 1.4 %hand_over.1 = (bf16[128,128]{1,0:T(8,128)(2,1)}, f32[1,128]{1,0:T(1,128)}) custom-call(bf16[128,128]{1,0:T(8,128)(2,1)} %get-tuple-element.6.layer, f32[1,128]{1,0:T(1,128)} %get-tuple-element.7.loss), custom_call_target="tpu_custom_call" | custom-call | tf_op jit(solution)/shard_map/hand_over/pallas_call | solution.py:441

commit v3 on v2

--- a/solution.py
+++ b/solution.py
@@ -50,7 +50,7 @@
     queries, response_keys, response_values, prompt_keys, prompt_values, length, residual_in,
     out_weight, gain_in, vocab_weight, targets_in,
     layer_out, row_loss,
-    residual, gain, targets, spread, small, resp, respbuf, kbuf, vbuf, qbuf, ostage, sstage, rbuf, rstat, mrg, abuf, wbuf,
+    residual, gain, targets, spread, small, resp, respbuf, kbuf, kt, vbuf, qbuf, ostage, sstage, rbuf, rstat, mrg, abuf, wbuf,
     pown, ppart, gbuf, ssbuf, ssplane, wv, acc, fbuf,
     local_sem, vocab_sem, kv_recv, w_recv, small_recv, q_ring, q_diag, r_recv, own_sem, a_recv,
     p_recv, g_ring, g_diag, h_recv, s_recv, f_recv, send_sem,
@@ -87,14 +87,21 @@
 
     own_copies = [
         pltpu.make_async_copy(prompt_keys.at[:, my_cols], kbuf.at[c], local_sem.at[0]),
-        pltpu.make_async_copy(prompt_values.at[:, my_cols], vbuf.at[c], local_sem.at[1]),
-        pltpu.make_async_copy(out_weight.at[my_half, :], wbuf.at[:, w_lane], local_sem.at[2]),
+        pltpu.make_async_copy(out_weight.at[my_half, :], wbuf.at[:, w_lane], local_sem.at[1]),
         pltpu.make_async_copy(residual_in, residual, local_sem.at[3]),
         pltpu.make_async_copy(gain_in, gain, local_sem.at[4]),
         pltpu.make_async_copy(targets_in, targets, local_sem.at[5]),
     ]
-    for copy in own_copies:
+    value_copies = [
+        pltpu.make_async_copy(
+            prompt_values.at[:, pl.ds(pl.multiple_of(c * 256 + j * 128, 128), 128)],
+            vbuf.at[j, c, :, pl.ds(0, 128)], local_sem.at[6 + j],
+        )
+        for j in range(2)
+    ]
+    for copy in own_copies + value_copies:
         copy.start()
+    vbuf[:, :, :, 128:] = jnp.ones((2, 2, KEYS_DEV, 128), BF16)
     vocab_copies = [
         pltpu.make_async_copy(
             vocab_weight.at[pl.ds(i * 1024, 1024), :], wv.at[pl.ds(i * 1024, 1024), :],
@@ -132,7 +139,18 @@
             send(heads, mine, q_ring.at[0, 4 - d], device(z, turn(x, d), core), 0)
             send(heads, mine, q_ring.at[1, 4 - d], device(turn(z, d), x, core), 0)
     send(prompt_keys.at[:, other_cols], kbuf.at[c], kv_recv.at[0], sibling, 2)
-    send(prompt_values.at[:, other_cols], vbuf.at[c], kv_recv.at[1], sibling, 2)
+    for j in range(2):
+        send(
+            prompt_values.at[:, pl.ds(pl.multiple_of(other * 256 + j * 128, 128), 128)],
+            vbuf.at[j, c, :, pl.ds(0, 128)], kv_recv.at[1 + j], sibling, 2,
+        )
+
+    def turn_keys(core):
+        for j in range(2):
+            kt[j, core] = kbuf[core, :, j * 128 : (j + 1) * 128].T
+
+    own_copies[0].wait()
+    turn_keys(c)
     for d in (1, 3, 2):
         sx, sz = turn(x, d), turn(z, d)
         drain(qbuf.at[0, 0, pl.ds(0, 128), :], q_ring.at[0, d])
@@ -154,10 +172,11 @@
     key_ok = (key_column % 16 < 4) & (key_id < live)
     row_in_plane = lax.broadcasted_iota(jnp.int32, (256, 32), 0) // 8
     drain(resp.at[pl.ds(0, 2)], small_recv.at[0])
-    own_copies[0].wait()
     drain(kbuf.at[0], kv_recv.at[0])
-    own_copies[1].wait()
-    drain(vbuf.at[0], kv_recv.at[1])
+    turn_keys(other)
+    for j in range(2):
+        value_copies[j].wait()
+        drain(vbuf.at[0, 0, :, pl.ds(0, 128)], kv_recv.at[1 + j])
 
     def with_ones(v):
         return jnp.concatenate([v, jnp.ones_like(v)], 1)
@@ -171,10 +190,9 @@
 
         visible = key_ok & (key_id <= t * 32 + row_in_plane)
         for j in range(2):
-            cols = slice(j * 128, (j + 1) * 128)
             q = qbuf[t, j]
-            s0 = dot_nt(q, kbuf[0, :, cols])
-            s1 = dot_nt(q, kbuf[1, :, cols])
+            s0 = dot_nn(q, kt[j, 0])
+            s1 = dot_nn(q, kt[j, 1])
             resp_keys = jnp.concatenate([respbuf[0, j, 0:16, :], respbuf[1, j, 0:16, :]], 0)
             resp_values = jnp.concatenate([respbuf[0, j, 16:32, :], respbuf[1, j, 16:32, :]], 0)
             sr = jnp.where(visible, dot_nt(q, resp_keys), -jnp.inf)
@@ -186,8 +204,8 @@
             p1 = jnp.exp2(s1 * SCORE_SCALE - peak)
             pr = jnp.exp2(sr * SCORE_SCALE - peak)
             o = (
-                dot_nn(p0.astype(BF16), with_ones(vbuf[0, :, cols]))
-                + dot_nn(p1.astype(BF16), with_ones(vbuf[1, :, cols]))
+                dot_nn(p0.astype(BF16), vbuf[j, 0])
+                + dot_nn(p1.astype(BF16), vbuf[j, 1])
                 + dot_nn(pr.astype(BF16), with_ones(resp_values))
             )
             total = o[:, 128:]
@@ -196,24 +214,25 @@
                 rows = slice(half * 128, (half + 1) * 128)
                 sstage[u, j, half, 0:1, :] = to_row(peak[rows])
                 sstage[u, j, half, 1:2, :] = to_row(total[rows])
-                quarter = 2 * half + j
-                owner = device(t, quarter, c)
-                part = ostage.at[u, j, pl.ds(half * 128, 128), :]
-                stat = sstage.at[u, j, half]
-
-                def to_owner():
-                    send(part, rbuf.at[chip], r_recv.at[0], owner, 4)
-                    send(stat, rstat.at[chip], r_recv.at[1], owner, 5)
-
-                if u > 0:
-                    to_owner()
-                    continue
-                pl.when(owner != me)(to_owner)
-
-                @pl.when(owner == me)
-                def _():
-                    pltpu.make_async_copy(part, rbuf.at[chip], own_sem.at[0]).start()
-                    pltpu.make_async_copy(stat, rstat.at[chip], own_sem.at[1]).start()
+        for quarter in range(4):
+            half, j = quarter // 2, quarter % 2
+            owner = device(t, quarter, c)
+            part = ostage.at[u, j, pl.ds(half * 128, 128), :]
+            stat = sstage.at[u, j, half]
+
+            def to_owner():
+                send(part, rbuf.at[chip], r_recv.at[0], owner, 4)
+                send(stat, rstat.at[chip], r_recv.at[1], owner, 5)
+
+            if u > 0:
+                to_owner()
+                continue
+            pl.when(owner != me)(to_owner)
+
+            @pl.when(owner == me)
+            def _():
+                pltpu.make_async_copy(part, rbuf.at[chip], own_sem.at[0]).start()
+                pltpu.make_async_copy(stat, rstat.at[chip], own_sem.at[1]).start()
 
     drain(rstat.at[pl.ds(0, 15)], r_recv.at[1])
     drain(rstat.at[0], own_sem.at[1])
@@ -236,7 +255,7 @@
     far_first = sorted([(dz, dx) for dz in range(4) for dx in range(4)], key=lambda d: -torus_distance(d))
     for dz, dx in far_first[:-1]:
         send(abuf.at[z, x], abuf.at[z, x], a_recv.at[0], device(turn(z, dz), turn(x, dx), c), 6)
-    for copy in own_copies[2:]:
+    for copy in own_copies[1:]:
         copy.wait()
     drain(wbuf.at[:, pl.ds(0, 128)], w_recv.at[0])
     drain(rbuf.at[pl.ds(0, 15)], a_recv.at[0])
@@ -258,10 +277,11 @@
     gbuf[z, x, c] = (layer * gain[...]).astype(BF16)
     ssbuf[x * 2 + c] = to_row(jnp.sum(layer * layer, 1, keepdims=True))
 
-    def gather(full, half, ring, diag, kind, on_ring):
+    def gather(full, half, ring, diag, kind, first_sent, on_ring):
         for d in (1, 3, 2):
             send(full(z, x), full(z, x), ring.at[0, 4 - d], device(z, turn(x, d), c), kind)
             send(full(z, x), full(z, x), ring.at[1, 4 - d], device(turn(z, d), x, c), kind)
+        first_sent()
         for d in (1, 3, 2):
             sx, sz = turn(x, d), turn(z, d)
             drain(full(0, 0), ring.at[0, d])
@@ -284,11 +304,13 @@
     def to_sibling(cz, cx, index):
         send(g_full(cz, cx), g_full(cz, cx), h_recv.at[index], sibling, 9)
 
-    to_sibling(z, x, 0)
-    for peer in x_peers + [sibling]:
-        mine = ssbuf.at[x * 2 + c]
-        send(mine, mine, s_recv.at[0], peer, 10)
-    gather(g_full, g_half, g_ring, g_diag, 8, to_sibling)
+    def first_sent():
+        to_sibling(z, x, 0)
+        for peer in x_peers + [sibling]:
+            mine = ssbuf.at[x * 2 + c]
+            send(mine, mine, s_recv.at[0], peer, 10)
+
+    gather(g_full, g_half, g_ring, g_diag, 8, first_sent, to_sibling)
     drain(ssbuf.at[pl.ds(0, 7)], s_recv.at[0])
     ssplane[z] = jnp.sum(ssbuf[:, 0, :], 0, keepdims=True)
     for d in (2, 1, 3):
@@ -395,7 +417,8 @@
             pltpu.VMEM((4, 32, 128), BF16),
             pltpu.VMEM((2, 2, 32, 128), BF16),
             pltpu.VMEM((2, KEYS_DEV, 256), BF16),
-            pltpu.VMEM((2, KEYS_DEV, 256), BF16),
+            pltpu.VMEM((2, 2, 128, KEYS_DEV), BF16),
+            pltpu.VMEM((2, 2, KEYS_DEV, 256), BF16),
             pltpu.VMEM((4, 2, 256, 128), BF16),
             pltpu.VMEM((4, 2, 256, 128), BF16),
             pltpu.VMEM((4, 2, 2, 8, 128), F32),
@@ -412,9 +435,9 @@
             pltpu.VMEM((D, VOCAB_DEV), BF16),
             pltpu.VMEM((ROWS, VOCAB_DEV), F32),
             pltpu.VMEM((32, 1, 384), F32),
-            dma((6,)),
+            dma((8,)),
             dma((4,)),
-            dma((2,)),
+            dma((3,)),
             dma((1,)),
             dma((1,)),
             dma((2, 4)),

time: 59.7 us -> 58.5 us (0.980)
  Pallas kernels: 58.2 us -> 57 us
    pallas_call x1, Pallas kernels: 56.8 us -> 55.6 us  [local(): pl.pallas_call(kernel, out_shape=shapes, in_specs=[vmem, vmem, vmem, hbm,...]
where the time goes in v3:
time: 58.5 us; the launch traced here: 58.2 us
  Pallas kernels  57 us (97%)
  between operations  1.29 us (2%)
    pallas_call x1, Pallas kernels, local(): pl.pallas_call(kernel, out_shape=shapes, in_specs=[vmem, vmem, vmem, hbm,...  55.6 us
    pallas_call x1, Pallas kernels, local(): pl.pallas_call(hand_over, out_shape=shapes, in_specs=[vmem, vmem], out_sp...  1.38 us

profile of v3, /device:TPU:1, one launch (start us, length us, event | category | flops | bytes accessed | tf_op | source)
XLA Modules:
  0.0 58.2 jit_solution(6262134657493850783)
XLA Ops:
  1.3 55.6 %score_response.1 = (bf16[128,128]{1,0:T(8,128)(2,1)}, f32[1,128]{1,0:T(1,128)}) custom-call(bf16[4,4096]{1,0:T(4,128)(2,1)} %queries.1, bf16[4,512]{1,0:T(4,128)(2,1)} %response_keys.1, bf16[4,512]{1,0:T(4,128)(2,1)} %response_values.1, bf16[1024,512]{1,0:T(8,128)(2,1)} %prompt_keys.1, bf16[1024,512]{1,0:T(8,128)(2,1)} %prompt_values.1, s32[1]{0:T(128)S(6)} %copy.13.length, ...), custom_call_target="tpu_custom_call" | custom-call | tf_op jit(solution)/shard_map/score_response/pallas_call | solution.py:403
  56.9 1.4 %hand_over.1 = (bf16[128,128]{1,0:T(8,128)(2,1)}, f32[1,128]{1,0:T(1,128)}) custom-call(bf16[128,128]{1,0:T(8,128)(2,1)} %get-tuple-element.6.layer, f32[1,128]{1,0:T(1,128)} %get-tuple-element.7.loss), custom_call_target="tpu_custom_call" | custom-call | tf_op jit(solution)/shard_map/hand_over/pallas_call | solution.py:464

commit v4 on v3

--- a/solution.py
+++ b/solution.py
@@ -259,16 +259,20 @@
         copy.wait()
     drain(wbuf.at[:, pl.ds(0, 128)], w_recv.at[0])
     drain(rbuf.at[pl.ds(0, 15)], a_recv.at[0])
-    projected = None
-    for j in range(2):
-        attn = jnp.concatenate(
-            [abuf[t, 2 * half + j] for t in range(4) for half in range(2)], 0
+    attn = [
+        jnp.concatenate([abuf[t, 2 * half + j] for t in range(4) for half in range(2)], 0)
+        for j in range(2)
+    ]
+
+    def project(columns):
+        lanes = pl.ds(pl.multiple_of(columns * 128, 128), 128)
+        return dot_nn(attn[0], wbuf[pl.ds(0, 1024), lanes]) + dot_nn(
+            attn[1], wbuf[pl.ds(1024, 1024), lanes]
         )
-        term = dot_nn(attn, wbuf[pl.ds(j * 1024, 1024), :])
-        projected = term if j == 0 else projected + term
-    pown[0] = projected[:, :128]
-    pown[1] = projected[:, 128:]
+
+    pown[other] = project(other)
     send(pown.at[other], ppart, p_recv.at[0], sibling, 7)
+    pown[c] = project(c)
     base = residual[...].astype(F32) + pown[c]
     drain(ppart, p_recv.at[0])
     layer = (base + ppart[...]).astype(BF16)

time: 58.5 us -> 57.2 us (0.978)
  Pallas kernels: 57 us -> 55.7 us
    pallas_call x1, Pallas kernels: 55.6 us -> 54.3 us  [local(): pl.pallas_call(kernel, out_shape=shapes, in_specs=[vmem, vmem, vmem, hbm,...]
where the time goes in v4:
time: 57.2 us; the launch traced here: 56.9 us
  Pallas kernels  55.7 us (97%)
  between operations  1.29 us (2%)
    pallas_call x1, Pallas kernels, local(): pl.pallas_call(kernel, out_shape=shapes, in_specs=[vmem, vmem, vmem, hbm,...  54.3 us
    pallas_call x1, Pallas kernels, local(): pl.pallas_call(hand_over, out_shape=shapes, in_specs=[vmem, vmem], out_sp...  1.38 us

profile of v4, /device:TPU:1, one launch (start us, length us, event | category | flops | bytes accessed | tf_op | source)
XLA Modules:
  0.0 56.9 jit_solution(5214012952027809013)
XLA Ops:
  1.3 54.3 %score_response.1 = (bf16[128,128]{1,0:T(8,128)(2,1)}, f32[1,128]{1,0:T(1,128)}) custom-call(bf16[4,4096]{1,0:T(4,128)(2,1)} %queries.1, bf16[4,512]{1,0:T(4,128)(2,1)} %response_keys.1, bf16[4,512]{1,0:T(4,128)(2,1)} %response_values.1, bf16[1024,512]{1,0:T(8,128)(2,1)} %prompt_keys.1, bf16[1024,512]{1,0:T(8,128)(2,1)} %prompt_values.1, s32[1]{0:T(128)S(6)} %copy.13.length, ...), custom_call_target="tpu_custom_call" | custom-call | tf_op jit(solution)/shard_map/score_response/pallas_call | solution.py:407
  55.6 1.4 %hand_over.1 = (bf16[128,128]{1,0:T(8,128)(2,1)}, f32[1,128]{1,0:T(1,128)}) custom-call(bf16[128,128]{1,0:T(8,128)(2,1)} %get-tuple-element.6.layer, f32[1,128]{1,0:T(1,128)} %get-tuple-element.7.loss), custom_call_target="tpu_custom_call" | custom-call | tf_op jit(solution)/shard_map/hand_over/pallas_call | solution.py:468

commit v5 on v4

--- a/solution.py
+++ b/solution.py
@@ -151,6 +151,8 @@
 
     own_copies[0].wait()
     turn_keys(c)
+    drain(kbuf.at[0], kv_recv.at[0])
+    turn_keys(other)
     for d in (1, 3, 2):
         sx, sz = turn(x, d), turn(z, d)
         drain(qbuf.at[0, 0, pl.ds(0, 128), :], q_ring.at[0, d])
@@ -172,8 +174,6 @@
     key_ok = (key_column % 16 < 4) & (key_id < live)
     row_in_plane = lax.broadcasted_iota(jnp.int32, (256, 32), 0) // 8
     drain(resp.at[pl.ds(0, 2)], small_recv.at[0])
-    drain(kbuf.at[0], kv_recv.at[0])
-    turn_keys(other)
     for j in range(2):
         value_copies[j].wait()
         drain(vbuf.at[0, 0, :, pl.ds(0, 128)], kv_recv.at[1 + j])

time: 57.2 us -> 57.4 us (level)
  no operation moved by 1% of the time
where the time goes in v5:
time: 57.4 us; the launch traced here: 57.1 us
  Pallas kernels  55.8 us (97%)
  between operations  1.29 us (2%)
    pallas_call x1, Pallas kernels, local(): pl.pallas_call(kernel, out_shape=shapes, in_specs=[vmem, vmem, vmem, hbm,...  54.5 us
    pallas_call x1, Pallas kernels, local(): pl.pallas_call(hand_over, out_shape=shapes, in_specs=[vmem, vmem], out_sp...  1.38 us

profile of v5, /device:TPU:1, one launch (start us, length us, event | category | flops | bytes accessed | tf_op | source)
XLA Modules:
  0.0 57.1 jit_solution(3437472551656452013)
XLA Ops:
  1.3 54.5 %score_response.1 = (bf16[128,128]{1,0:T(8,128)(2,1)}, f32[1,128]{1,0:T(1,128)}) custom-call(bf16[4,4096]{1,0:T(4,128)(2,1)} %queries.1, bf16[4,512]{1,0:T(4,128)(2,1)} %response_keys.1, bf16[4,512]{1,0:T(4,128)(2,1)} %response_values.1, bf16[1024,512]{1,0:T(8,128)(2,1)} %prompt_keys.1, bf16[1024,512]{1,0:T(8,128)(2,1)} %prompt_values.1, s32[1]{0:T(128)S(6)} %copy.13.length, ...), custom_call_target="tpu_custom_call" | custom-call | tf_op jit(solution)/shard_map/score_response/pallas_call | solution.py:407
  55.7 1.4 %hand_over.1 = (bf16[128,128]{1,0:T(8,128)(2,1)}, f32[1,128]{1,0:T(1,128)}) custom-call(bf16[128,128]{1,0:T(8,128)(2,1)} %get-tuple-element.6.layer, f32[1,128]{1,0:T(1,128)} %get-tuple-element.7.loss), custom_call_target="tpu_custom_call" | custom-call | tf_op jit(solution)/shard_map/hand_over/pallas_call | solution.py:468
